TPU v7x, 32 devices: a whole 2x2x4 slice. The times are simulated.
32 devices in a mesh: tgt: 16 (over z, y, core), src: 2 (over x).
Axes of the slice: x: 2, y: 2, z: 4, core: 2. Of those that a mesh axis runs over, the one named last changes fastest.
Arguments:
- tgt_points: bfloat16 [3, 8192], P(None, 'tgt'), may hold values from -4 to 4
- tgt_weight: float32 [8192], P('tgt'), may hold values from 0.5 to 2
- src_points: bfloat16 [4, 3, 4096], P(None, None, ('tgt', 'src')), may hold values from -4 to 4
- src_weight: float32 [4, 4096], P(None, ('tgt', 'src')), may hold values from 0.5 to 2
- basis: float32 [4, 3, 4096], P(None, None, ('tgt', 'src')), may hold values from 0.05 to 1
- span: int32 [4, 4096], P(None, ('tgt', 'src')), may hold values from 0 to 29
- patch: int32 [4, 4096], P(None, ('tgt', 'src')), may hold values from 0 to 3
- patch_factor: float32 [4, 2, 128], P(None, None, ('tgt', 'src')), may hold values from -1.5 to 1.5
- ctrl_weight: float32 [4, 1024], P(None, ('tgt', 'src')), may hold values from 0.5 to 2
- ctrl_coef: bfloat16 [4, 128, 1024], P(None, None, ('tgt', 'src')), may hold values from -6 to 6
- band: float32 [8, 8192], P(None, 'tgt'), may hold values from -0.5 to 0.5
- offsets: int32 [8], replicated, may hold values from -8 to 8, as said below
Outputs:
- shell_field: float32 [8192, 128], P('tgt')
Inputs may be any that keep to these rules, and one draw needn't show every extreme that they name: span of source point j is local to the 32 control points of the block j // 128. patch of source point j is local to the 4 patches of the block j // 128. offsets[0] is 8 and offsets[1] is -8.
All inputs are finite; a program needn't handle non-finite values.
Results may differ from a plain program's by a relative error of at most 0.0041.
Values may be sent and summed in bfloat16 or wider, within the bound.
A program may use at most 128 MiB of HBM per device.

v0:
```python
import functools
import math

import jax
import jax.numpy as jnp
from jax import lax
from jax.experimental import pallas as pl
from jax.experimental.pallas import tpu as pltpu
from jax.sharding import PartitionSpec as P

HALO = 8
WAVE = 8.0
SMOOTH = 0.0025
OMEGA = WAVE / (2.0 * math.pi)
KAPPA = OMEGA * OMEGA
MAGIC = 12582912.0

F32 = jnp.float32
BF16 = jnp.bfloat16
MESH = pl.DeviceIdType.MESH


def pieces(value):
    high = value.astype(BF16).astype(F32)
    rest = value - high
    mid = rest.astype(BF16).astype(F32)
    return high, mid, (rest - mid).astype(BF16).astype(F32)


def flip(index, bits):
    out = index
    place = 1
    while place <= bits:
        if bits // place % 2:
            out = out + (1 - 2 * ((index // place) % 2)) * place
        place *= 2
    return out


def target_rows(points):
    square = KAPPA * (
        points[0:1] * points[0:1] + points[1:2] * points[1:2] + points[2:3] * points[2:3]
    )
    high, mid, low = pieces(square)
    one = jnp.ones_like(square)
    return jnp.concatenate(
        [points, points, points, high, mid, low, one, one, one, jnp.zeros_like(one)], axis=0
    )


def source_rows(points):
    square = KAPPA * (
        SMOOTH
        + points[0:1] * points[0:1]
        + points[1:2] * points[1:2]
        + points[2:3] * points[2:3]
    )
    high, mid, low = pieces(square)
    ph, pm, plo = pieces(points * (-2.0 * KAPPA))
    one = jnp.ones_like(square)
    return jnp.concatenate(
        [ph, pm, plo, one, one, one, high, mid, low, jnp.zeros_like(one)], axis=0
    )


SIN = (4.441527135827024, -7.264541902232219, 3.2516001820136307)
COS = (1.4133599520203266, -6.916869803046874, 5.067054327781224)


def wave_terms(square):
    inv = lax.rsqrt(square)
    turns = square * inv
    frac = turns - ((turns + MAGIC) - MAGIC)
    z = frac * frac
    half_sin = frac * (SIN[0] + z * (SIN[1] + z * SIN[2]))
    half_cos = COS[0] + z * (COS[1] + z * COS[2])
    prod = half_sin * inv
    return inv - half_sin * prod, prod * half_cos


def body(
    n_tgt,
    n_src,
    scale,
    tgt_ref,
    tw_ref,
    src_ref,
    sw_ref,
    basis_ref,
    span_ref,
    patch_ref,
    pf_ref,
    cw_ref,
    coef_ref,
    band_ref,
    off_ref,
    out_ref,
    gather,
    taug,
    bw,
    hal_own,
    hal_in,
    hw,
    saug_a,
    saug_b,
    dens_a,
    dens_b,
    kern0,
    kern1,
    kern2,
    acc,
    part,
    peers,
    pot,
    send_sem,
    recv_sem,
    hsend,
    hrecv,
    psend,
    precv,
):
    me = lax.axis_index("tgt")
    sme = lax.axis_index("src")
    rows = tgt_ref.shape[1]
    rounds, fields2, ctrl = coef_ref.shape
    half = fields2 // 2
    count = sw_ref.shape[1]
    odd = me % 2
    up = (me + 1) % n_tgt
    down = (me + n_tgt - 1) % n_tgt
    other = (me + n_tgt - 1 + 2 * odd) % n_tgt

    barrier = pltpu.get_barrier_semaphore()
    greeted = 0
    for bits in [1] + list(range(2, n_tgt, 2)):
        pl.semaphore_signal(
            barrier, inc=1, device_id=(flip(me, bits), sme), device_id_type=MESH
        )
        greeted += 1
    pl.semaphore_signal(barrier, inc=1, device_id=(other, sme), device_id_type=MESH)
    greeted += 1
    for bits in range(1, n_src):
        pl.semaphore_signal(
            barrier, inc=1, device_id=(me, flip(sme, bits)), device_id_type=MESH
        )
        greeted += 1

    gather[0, 0:fields2, :] = jnp.concatenate(
        [coef_ref[r].astype(F32) for r in range(rounds)], axis=1
    ).astype(BF16)
    for r in range(rounds):
        span = span_ref[r : r + 1, :]
        index = jnp.broadcast_to(span, (8, count)) + lax.broadcasted_iota(
            jnp.int32, (8, count), 0
        )
        weights = jnp.zeros((8, count), F32)
        for c in range(ctrl):
            weights = jnp.where(index == c, cw_ref[r, c], weights)
        scaled = basis_ref[r] * weights[0:3]
        denom = scaled[0:1] + scaled[1:2] + scaled[2:3]
        scaled = scaled * (sw_ref[r : r + 1, :] / denom)
        patch = patch_ref[r : r + 1, :]
        fre = jnp.zeros((1, count), F32)
        fim = jnp.zeros((1, count), F32)
        for p in range(pf_ref.shape[2]):
            fre = jnp.where(patch == p, pf_ref[r, 0, p], fre)
            fim = jnp.where(patch == p, pf_ref[r, 1, p], fim)
        frh, frl, _ = pieces(fre)
        fih, fil, _ = pieces(fim)
        sh, sl, _ = pieces(scaled)
        meta = jnp.concatenate(
            [
                src_ref[r].astype(F32),
                span.astype(F32),
                frh,
                frl,
                fih,
                fil,
                sh,
                sl,
                jnp.zeros((2, count), F32),
            ],
            axis=0,
        )
        gather[0, fields2 + 16 * r : fields2 + 16 * (r + 1), :] = meta.astype(BF16)

    points = tgt_ref[...].astype(F32)
    tweight = tw_ref[...]
    strip = jnp.concatenate([points, tweight, jnp.zeros((4, rows), F32)], axis=0)
    hal_own[0] = strip[:, 0:128]
    hal_own[1] = strip[:, rows - 128 : rows]

    pl.semaphore_wait(barrier, greeted)

    def direct(bits):
        return pltpu.make_async_remote_copy(
            src_ref=gather.at[0],
            dst_ref=gather.at[bits],
            send_sem=send_sem.at[bits],
            recv_sem=recv_sem.at[bits],
            device_id=(flip(me, bits), sme),
            device_id_type=MESH,
        )

    def forward(slot):
        return pltpu.make_async_remote_copy(
            src_ref=gather.at[slot],
            dst_ref=gather.at[slot + 1],
            send_sem=send_sem.at[slot + 1],
            recv_sem=recv_sem.at[slot + 1],
            device_id=(flip(me, 1), sme),
            device_id_type=MESH,
        )

    forward(0).start()
    for bits in range(2, n_tgt, 2):
        direct(bits).start()
    halo_up = pltpu.make_async_remote_copy(
        src_ref=hal_own.at[1],
        dst_ref=hal_in.at[0],
        send_sem=hsend.at[0],
        recv_sem=hrecv.at[0],
        device_id=(up, sme),
        device_id_type=MESH,
    )
    halo_down = pltpu.make_async_remote_copy(
        src_ref=hal_own.at[0],
        dst_ref=hal_in.at[1],
        send_sem=hsend.at[1],
        recv_sem=hrecv.at[1],
        device_id=(down, sme),
        device_id_type=MESH,
    )
    halo_up.start()
    halo_down.start()

    taug[0:rows, :] = jnp.transpose(target_rows(points)).astype(BF16)
    bw[...] = jnp.transpose(
        jnp.concatenate([band_ref[...], strip[3:4], jnp.zeros((7, rows), F32)], axis=0)
    )
    acc[...] = jnp.zeros_like(acc)
    halo_up.wait()
    halo_down.wait()
    low = hal_in[0]
    high = hal_in[1]
    low_t = jnp.transpose(target_rows(low[0:3]))
    high_t = jnp.transpose(target_rows(high[0:3]))
    taug[rows : rows + 16, :] = jnp.concatenate(
        [high_t[0:8], low_t[120:128]], axis=0
    ).astype(BF16)
    hw[0:8, :] = jnp.transpose(high)[0:8] * jnp.where(me < n_tgt - 1, 1.0, 0.0)
    hw[8:16, :] = jnp.transpose(low)[120:128] * jnp.where(me > 0, 1.0, 0.0)

    def prepare(slot, saug, dens):
        coef = gather[slot, 0:fields2, :]
        coef2 = jnp.concatenate([coef, coef], axis=1)
        label = lax.broadcasted_iota(jnp.int32, (ctrl, count), 0).astype(F32)
        for r in range(rounds):
            meta = gather[slot, fields2 + 16 * r : fields2 + 16 * (r + 1), :].astype(F32)
            saug[:, r * count : (r + 1) * count] = source_rows(meta[0:3]).astype(BF16)
            spread_h = jnp.zeros((ctrl, count), F32)
            spread_l = jnp.zeros((ctrl, count), F32)
            for a in range(3):
                hit = label == meta[3:4] + float(a)
                spread_h = jnp.where(hit, meta[8 + a : 9 + a], spread_h)
                spread_l = jnp.where(hit, meta[11 + a : 12 + a], spread_l)

            def placed(block):
                parts = [block.astype(BF16)]
                if r:
                    parts = [jnp.zeros((r * ctrl, count), BF16)] + parts
                if r < rounds - 1:
                    parts = parts + [jnp.zeros(((rounds - 1 - r) * ctrl, count), BF16)]
                return parts

            spread = jnp.concatenate(placed(spread_h) + placed(spread_l), axis=0)
            ratio = jnp.dot(coef2, spread, preferred_element_type=F32)
            fre = meta[4:5] + meta[5:6]
            fim = meta[6:7] + meta[7:8]
            re = fre * ratio[:half] - fim * ratio[half:]
            im = fre * ratio[half:] + fim * ratio[:half]
            at = r * count
            dens[0:half, at : at + count] = re.astype(BF16)
            dens[half:fields2, at : at + count] = im.astype(BF16)
            at = (rounds + r) * count
            dens[0:half, at : at + count] = (-im).astype(BF16)
            dens[half:fields2, at : at + count] = re.astype(BF16)

    kerns = (kern0, kern1, kern2)
    tile = (rows + 16) // 3
    width = rounds * count

    def apply(saug, dens):
        for m in range(3):
            kern = kerns[m]
            square = jnp.dot(
                taug[m * tile : (m + 1) * tile, :], saug[...], preferred_element_type=F32
            )
            for i in range(0, tile, 16):
                re, im = wave_terms(square[i : i + 16])
                kern[i : i + 16, 0:width] = re.astype(BF16)
                kern[i : i + 16, width : 2 * width] = im.astype(BF16)
            acc[m * tile : (m + 1) * tile, :] += lax.dot_general(
                kern[...], dens[...], (((1,), (1,)), ((), ())), preferred_element_type=F32
            )

    prepare(0, saug_a, dens_a)

    def pair(q, carry):
        slot = 2 * q
        forward(slot).wait_recv()
        prepare(slot + 1, saug_b, dens_b)
        apply(saug_a, dens_a)

        @pl.when(q < n_tgt // 2 - 1)
        def _():
            direct_recv(slot + 2).wait_recv()
            forward(slot + 2).start()
            prepare(slot + 2, saug_a, dens_a)

        apply(saug_b, dens_b)
        return carry

    def direct_recv(slot):
        return pltpu.make_async_remote_copy(
            src_ref=gather.at[0],
            dst_ref=gather.at[slot],
            send_sem=send_sem.at[slot],
            recv_sem=recv_sem.at[slot],
            device_id=(flip(me, 1), sme),
            device_id_type=MESH,
        )

    lax.fori_loop(0, n_tgt // 2, pair, 0)

    def share(bits, m):
        return pltpu.make_async_remote_copy(
            src_ref=part.at[pl.ds(m * tile, tile)],
            dst_ref=peers.at[bits, pl.ds(m * tile, tile)],
            send_sem=psend.at[bits, m],
            recv_sem=precv.at[bits, m],
            device_id=(me, flip(sme, bits)),
            device_id_type=MESH,
        )

    for m in range(3):
        part[m * tile : (m + 1) * tile, :] = acc[m * tile : (m + 1) * tile, :].astype(BF16)
        for bits in range(1, n_src):
            share(bits, m).start()

    for m in range(3):
        at = slice(m * tile, (m + 1) * tile)
        for bits in range(1, n_src):
            share(bits, m).wait_recv()
        terms = [part[at, :].astype(F32)]
        terms += [peers[bits, at, :].astype(F32) for bits in range(1, n_src)]
        while len(terms) > 1:
            terms = [terms[k] + terms[k + 1] for k in range(0, len(terms), 2)]
        acc[at, :] = terms[0] * scale

    pot[HALO : HALO + rows, :] = acc[0:rows, :] * bw[:, 8:9]
    pot[HALO + rows : HALO + rows + 8, :] = acc[rows : rows + 8, :] * hw[0:8, 3:4]
    pot[0:HALO, :] = acc[rows + 8 : rows + 16, :] * hw[8:16, 3:4]
    for start in range(0, rows, 128):
        value = pot[HALO + start : HALO + start + 128, :]
        for d in range(band_ref.shape[0]):
            shifted = pot[pl.ds(HALO + start + off_ref[d], 128), :]
            value = value + bw[start : start + 128, d : d + 1] * shifted
        out_ref[start : start + 128, :] = value

    for bits in range(1, n_tgt):
        direct_recv(bits).wait_send()
    for m in range(3):
        for bits in range(1, n_src):
            share(bits, m).wait_send()


def per_device(n_tgt, n_src, tgt_points, tgt_weight, src_points, src_weight, basis, span,
               patch, patch_factor, ctrl_weight, ctrl_coef, band, offsets):
    rows = tgt_points.shape[1]
    rounds, fields2, ctrl = ctrl_coef.shape
    count = src_weight.shape[1]
    sources = rounds * count * n_tgt * n_src
    scale = OMEGA / math.sqrt(sources)
    total = rows + 16
    width = rounds * count
    vmem = pl.BlockSpec(memory_space=pltpu.VMEM)
    smem = pl.BlockSpec(memory_space=pltpu.SMEM)
    return pl.pallas_call(
        functools.partial(body, n_tgt, n_src, scale),
        out_shape=jax.ShapeDtypeStruct((rows, fields2), F32),
        in_specs=[vmem] * 7 + [smem, smem, vmem, vmem, smem],
        out_specs=vmem,
        scratch_shapes=[
            pltpu.VMEM((n_tgt, fields2 + 16 * rounds, rounds * ctrl), BF16),
            pltpu.VMEM((total, 16), BF16),
            pltpu.VMEM((rows, 16), F32),
            pltpu.VMEM((2, 8, 128), F32),
            pltpu.VMEM((2, 8, 128), F32),
            pltpu.VMEM((16, 8), F32),
            pltpu.VMEM((16, width), BF16),
            pltpu.VMEM((16, width), BF16),
            pltpu.VMEM((fields2, 2 * width), BF16),
            pltpu.VMEM((fields2, 2 * width), BF16),
            pltpu.VMEM((total // 3, 2 * width), BF16),
            pltpu.VMEM((total // 3, 2 * width), BF16),
            pltpu.VMEM((total // 3, 2 * width), BF16),
            pltpu.VMEM((total, fields2), F32),
            pltpu.VMEM((total, fields2), BF16),
            pltpu.VMEM((n_src, total, fields2), BF16),
            pltpu.VMEM((total, fields2), F32),
            pltpu.SemaphoreType.DMA((n_tgt,)),
            pltpu.SemaphoreType.DMA((n_tgt,)),
            pltpu.SemaphoreType.DMA((2,)),
            pltpu.SemaphoreType.DMA((2,)),
            pltpu.SemaphoreType.DMA((n_src, 3)),
            pltpu.SemaphoreType.DMA((n_src, 3)),
        ],
        compiler_params=pltpu.CompilerParams(
            collective_id=0, has_side_effects=True, vmem_limit_bytes=40 * 1024 * 1024
        ),
    )(
        tgt_points,
        tgt_weight.reshape(1, rows),
        src_points,
        src_weight,
        basis,
        span,
        patch,
        patch_factor,
        ctrl_weight,
        ctrl_coef,
        band,
        offsets,
    )


def solution(mesh):
    in_specs = (
        P(None, "tgt"),
        P("tgt"),
        P(None, None, ("tgt", "src")),
        P(None, ("tgt", "src")),
        P(None, None, ("tgt", "src")),
        P(None, ("tgt", "src")),
        P(None, ("tgt", "src")),
        P(None, None, ("tgt", "src")),
        P(None, ("tgt", "src")),
        P(None, None, ("tgt", "src")),
        P(None, "tgt"),
        P(),
    )
    return jax.shard_map(
        functools.partial(per_device, mesh.shape["tgt"], mesh.shape["src"]),
        mesh=mesh,
        in_specs=in_specs,
        out_specs=P("tgt", None),
        check_vma=False,
    )
```

profile of v0, /device:TPU:0, one launch (start us, length us, event | category | flops | bytes accessed | tf_op | source)
XLA Modules:
  0.0 48.6 jit_solution(8423271297889085164)
XLA Ops:
  0.0 0.0 copy-start.9
  0.0 0.7 %copy.13.src_ref = bf16[4,3,128]{2,1,0:T(4,128)(2,1)S(1)} copy(bf16[4,3,128]{2,0,1:T(4,128)(2,1)} %param.14) | data formatting | bytes 6144 | tf_op args[2]
  0.7 0.0 copy-done.9
  0.7 0.0 copy-start
  0.7 0.0 copy-start.1
  0.7 0.0 copy-start.2
  0.7 0.0 copy-start.3
  0.8 0.0 copy-start.4
  0.8 0.0 copy-start.5
  0.8 0.0 copy-start.6
  0.8 0.0 copy-start.7
  0.8 0.0 copy-start.8
  0.8 0.9 %copy.15.coef_ref = bf16[4,128,32]{2,1,0:T(8,128)(2,1)S(1)} copy(bf16[4,128,32]{1,2,0:T(8,128)(2,1)} %param.21) | data formatting | bytes 65536 | tf_op args[9]
  1.7 0.0 copy-done
  1.7 0.0 copy-done.1
  1.8 0.0 copy-done.2
  1.8 0.0 copy-done.3
  1.8 0.0 copy-done.4
  1.8 0.0 copy-done.5
  1.8 0.0 copy-done.6
  1.8 0.0 copy-done.7
  1.8 0.0 copy-done.8
  1.8 46.0 %shard_map.118 = f32[512,128]{1,0:T(8,128)S(1)} custom-call(bf16[3,512]{1,0:T(4,128)(2,1)S(1)} %copy-done.1, f32[1,512]{1,0:T(1,128)S(1)} %bitcast.1, bf16[4,3,128]{2,1,0:T(4,128)(2,1)S(1)} %copy.13.src_ref, f32[4,128]{1,0:T(4,128)S(1)} %copy-done.4, f32[4,3,128]{2,1,0:T(4,128)S(1)} %copy.14.basis_ref, s32[4,128]{1,0:T(4,128)S(1)} %copy-done.5, ...), custom_call_target="tpu_custom_call" | custom-call | tf_op jit(solution)/shard_map/pallas_call | solution.py:389
  47.9 0.7 %copy.17 = f32[512,128]{1,0:T(8,128)} copy(f32[512,128]{1,0:T(8,128)S(1)} %shard_map.118) | data formatting | bytes 524288
  (1 shorter events, 0.0 us)
Async XLA Ops:
  0.0 0.7 %copy-start.9 = (f32[4,3,128]{2,0,1:T(4,128)S(1)}, f32[4,3,128]{2,0,1:T(4,128)}, u32[]{:S(2)}) copy-start(f32[4,3,128]{2,0,1:T(4,128)} %param.16) | copy-start | bytes 18436
  0.7 1.0 %copy-start = (f32[8,512]{1,0:T(8,128)S(1)}, f32[8,512]{1,0:T(8,128)}, u32[]{:S(2)}) copy-start(f32[8,512]{1,0:T(8,128)} %band_ref.1) | copy-start | bytes 49156
  0.7 1.0 %copy-start.1 = (bf16[3,512]{1,0:T(4,128)(2,1)S(1)}, bf16[3,512]{1,0:T(4,128)(2,1)}, u32[]{:S(2)}) copy-start(bf16[3,512]{1,0:T(4,128)(2,1)} %tgt_ref.1) | copy-start | bytes 9220
  0.7 1.0 %copy-start.2 = (f32[4,2,4]{2,1,0:T(2,128)S(1)}, f32[4,2,4]{2,1,0:T(2,128)}, u32[]{:S(2)}) copy-start(f32[4,2,4]{2,1,0:T(2,128)} %pf_ref.1) | copy-start | bytes 388
  0.7 1.0 %copy-start.3 = (f32[512]{0:T(512)S(1)}, f32[512]{0:T(512)}, u32[]{:S(2)}) copy-start(f32[512]{0:T(512)} %param.13) | copy-start | bytes 6148
  0.8 1.0 %copy-start.4 = (f32[4,128]{1,0:T(4,128)S(1)}, f32[4,128]{1,0:T(4,128)}, u32[]{:S(2)}) copy-start(f32[4,128]{1,0:T(4,128)} %sw_ref.1) | copy-start | bytes 6148
  0.8 1.0 %copy-start.5 = (s32[4,128]{1,0:T(4,128)S(1)}, s32[4,128]{1,0:T(4,128)}, u32[]{:S(2)}) copy-start(s32[4,128]{1,0:T(4,128)} %span_ref.1) | copy-start | bytes 6148
  0.8 1.0 %copy-start.6 = (s32[4,128]{1,0:T(4,128)S(1)}, s32[4,128]{1,0:T(4,128)}, u32[]{:S(2)}) copy-start(s32[4,128]{1,0:T(4,128)} %patch_ref.1) | copy-start | bytes 6148
  0.8 1.0 %copy-start.7 = (f32[4,32]{1,0:T(4,128)S(1)}, f32[4,32]{1,0:T(4,128)}, u32[]{:S(2)}) copy-start(f32[4,32]{1,0:T(4,128)} %cw_ref.1) | copy-start | bytes 1540
  0.8 1.0 %copy-start.8 = (s32[8]{0:T(128)S(1)}, s32[8]{0:T(128)}, u32[]{:S(2)}) copy-start(s32[8]{0:T(128)} %off_ref.1) | copy-start | bytes 100
where the time goes:
time: 48.9 us; the launch traced here: 48.6 us
  Pallas kernels  46 us (94%)
  local copies, waits for them, and re-layouts  2.38 us (5%)
    pallas_call x1, Pallas kernels, per_device(): pl.pallas_call(functools.partial(body, n_tgt, n_src, scale), out_shape=ja...  46 us
    unnamed x24, local copies, waits for them, and re-layouts  2.38 us

commit v1 on v0

--- a/solution.py
+++ b/solution.py
@@ -101,19 +101,22 @@
     hal_own,
     hal_in,
     hw,
-    saug_a,
-    saug_b,
-    dens_a,
-    dens_b,
+    saug,
+    dens,
     kern0,
     kern1,
     kern2,
+    kern3,
+    kern4,
+    kern5,
     acc,
     part,
     peers,
     pot,
     send_sem,
     recv_sem,
+    fsem,
+    gsem,
     hsend,
     hrecv,
     psend,
@@ -122,9 +125,11 @@
     me = lax.axis_index("tgt")
     sme = lax.axis_index("src")
     rows = tgt_ref.shape[1]
-    rounds, fields2, ctrl = coef_ref.shape
+    rounds, ctrl, fields2 = coef_ref.shape
     half = fields2 // 2
     count = sw_ref.shape[1]
+    base = rounds * ctrl
+    width = rounds * count
     odd = me % 2
     up = (me + 1) % n_tgt
     down = (me + n_tgt - 1) % n_tgt
@@ -145,10 +150,8 @@
         )
         greeted += 1
 
-    gather[0, 0:fields2, :] = jnp.concatenate(
-        [coef_ref[r].astype(F32) for r in range(rounds)], axis=1
-    ).astype(BF16)
     for r in range(rounds):
+        gather[0, ctrl * r : ctrl * (r + 1), :] = coef_ref[r]
         span = span_ref[r : r + 1, :]
         index = jnp.broadcast_to(span, (8, count)) + lax.broadcasted_iota(
             jnp.int32, (8, count), 0
@@ -165,24 +168,12 @@
         for p in range(pf_ref.shape[2]):
             fre = jnp.where(patch == p, pf_ref[r, 0, p], fre)
             fim = jnp.where(patch == p, pf_ref[r, 1, p], fim)
-        frh, frl, _ = pieces(fre)
-        fih, fil, _ = pieces(fim)
-        sh, sl, _ = pieces(scaled)
+        rh, rl, _ = pieces(scaled * fre)
+        ih, il, _ = pieces(scaled * fim)
         meta = jnp.concatenate(
-            [
-                src_ref[r].astype(F32),
-                span.astype(F32),
-                frh,
-                frl,
-                fih,
-                fil,
-                sh,
-                sl,
-                jnp.zeros((2, count), F32),
-            ],
-            axis=0,
-        )
-        gather[0, fields2 + 16 * r : fields2 + 16 * (r + 1), :] = meta.astype(BF16)
+            [src_ref[r].astype(F32), span.astype(F32), rh, rl, ih, il], axis=0
+        )
+        gather[0, base + 16 * r : base + 16 * (r + 1), :] = meta.astype(BF16)
 
     points = tgt_ref[...].astype(F32)
     tweight = tw_ref[...]
@@ -203,16 +194,26 @@
         )
 
     def forward(slot):
-        return pltpu.make_async_remote_copy(
-            src_ref=gather.at[slot],
-            dst_ref=gather.at[slot + 1],
-            send_sem=send_sem.at[slot + 1],
-            recv_sem=recv_sem.at[slot + 1],
-            device_id=(flip(me, 1), sme),
-            device_id_type=MESH,
-        )
-
-    forward(0).start()
+        return [
+            pltpu.make_async_remote_copy(
+                src_ref=ref.at[slot],
+                dst_ref=ref.at[slot + 1],
+                send_sem=sems.at[0, slot // 2],
+                recv_sem=sems.at[1, slot // 2],
+                device_id=(flip(me, 1), sme),
+                device_id_type=MESH,
+            )
+            for ref, sems in ((saug, fsem), (dens, gsem))
+        ]
+
+    def hand_on(slot):
+        for copy in forward(slot):
+            copy.start()
+
+    def handed(slot):
+        for copy in forward(slot):
+            copy.wait_recv()
+
     for bits in range(2, n_tgt, 2):
         direct(bits).start()
     halo_up = pltpu.make_async_remote_copy(
@@ -251,87 +252,83 @@
     hw[0:8, :] = jnp.transpose(high)[0:8] * jnp.where(me < n_tgt - 1, 1.0, 0.0)
     hw[8:16, :] = jnp.transpose(low)[120:128] * jnp.where(me > 0, 1.0, 0.0)
 
-    def prepare(slot, saug, dens):
-        coef = gather[slot, 0:fields2, :]
-        coef2 = jnp.concatenate([coef, coef], axis=1)
+    lane = lax.broadcasted_iota(jnp.int32, (1, fields2), 1)
+    sign = jnp.where(lane < half, -1.0, 1.0)
+
+    def turned(value):
+        return pltpu.roll(value, half, 1) * sign
+
+    def prepare(source, slot):
+        coef = gather[source, 0:base, :]
+        coef_i = turned(coef.astype(F32)).astype(BF16)
         label = lax.broadcasted_iota(jnp.int32, (ctrl, count), 0).astype(F32)
         for r in range(rounds):
-            meta = gather[slot, fields2 + 16 * r : fields2 + 16 * (r + 1), :].astype(F32)
-            saug[:, r * count : (r + 1) * count] = source_rows(meta[0:3]).astype(BF16)
-            spread_h = jnp.zeros((ctrl, count), F32)
-            spread_l = jnp.zeros((ctrl, count), F32)
-            for a in range(3):
-                hit = label == meta[3:4] + float(a)
-                spread_h = jnp.where(hit, meta[8 + a : 9 + a], spread_h)
-                spread_l = jnp.where(hit, meta[11 + a : 12 + a], spread_l)
-
-            def placed(block):
-                parts = [block.astype(BF16)]
-                if r:
-                    parts = [jnp.zeros((r * ctrl, count), BF16)] + parts
-                if r < rounds - 1:
-                    parts = parts + [jnp.zeros(((rounds - 1 - r) * ctrl, count), BF16)]
-                return parts
-
-            spread = jnp.concatenate(placed(spread_h) + placed(spread_l), axis=0)
-            ratio = jnp.dot(coef2, spread, preferred_element_type=F32)
-            fre = meta[4:5] + meta[5:6]
-            fim = meta[6:7] + meta[7:8]
-            re = fre * ratio[:half] - fim * ratio[half:]
-            im = fre * ratio[half:] + fim * ratio[:half]
-            at = r * count
-            dens[0:half, at : at + count] = re.astype(BF16)
-            dens[half:fields2, at : at + count] = im.astype(BF16)
-            at = (rounds + r) * count
-            dens[0:half, at : at + count] = (-im).astype(BF16)
-            dens[half:fields2, at : at + count] = re.astype(BF16)
-
-    kerns = (kern0, kern1, kern2)
+            meta = gather[source, base + 16 * r : base + 16 * (r + 1), :].astype(F32)
+            saug[slot, :, r * count : (r + 1) * count] = source_rows(meta[0:3]).astype(BF16)
+            hits = [label == meta[3:4] + float(a) for a in range(3)]
+            blocks = []
+            for kind in range(4):
+                block = jnp.zeros((ctrl, count), F32)
+                for a in range(3):
+                    row = 4 + 3 * kind + a
+                    block = jnp.where(hits[a], meta[row : row + 1], block)
+                blocks.append(block)
+            spread = jnp.transpose(jnp.concatenate(blocks, axis=0)).astype(BF16)
+            part_r = coef[ctrl * r : ctrl * (r + 1)]
+            part_i = coef_i[ctrl * r : ctrl * (r + 1)]
+            values = jnp.dot(
+                spread,
+                jnp.concatenate([part_r, part_r, part_i, part_i], axis=0),
+                preferred_element_type=F32,
+            )
+            dens[slot, r * count : (r + 1) * count, :] = values.astype(BF16)
+
     tile = (rows + 16) // 3
-    width = rounds * count
-
-    def apply(saug, dens):
-        for m in range(3):
-            kern = kerns[m]
-            square = jnp.dot(
-                taug[m * tile : (m + 1) * tile, :], saug[...], preferred_element_type=F32
-            )
+    kerns = (kern0, kern1, kern2, kern3, kern4, kern5)
+
+    def apply(first, blocks, m):
+        kre, kim = kerns[2 * m], kerns[2 * m + 1]
+        at = slice(m * tile, (m + 1) * tile)
+        for j in range(blocks):
+            square = jnp.dot(taug[at, :], saug[first + j], preferred_element_type=F32)
+            columns = slice(j * width, (j + 1) * width)
             for i in range(0, tile, 16):
                 re, im = wave_terms(square[i : i + 16])
-                kern[i : i + 16, 0:width] = re.astype(BF16)
-                kern[i : i + 16, width : 2 * width] = im.astype(BF16)
-            acc[m * tile : (m + 1) * tile, :] += lax.dot_general(
-                kern[...], dens[...], (((1,), (1,)), ((), ())), preferred_element_type=F32
-            )
-
-    prepare(0, saug_a, dens_a)
-
-    def pair(q, carry):
-        slot = 2 * q
-        forward(slot).wait_recv()
-        prepare(slot + 1, saug_b, dens_b)
-        apply(saug_a, dens_a)
-
-        @pl.when(q < n_tgt // 2 - 1)
-        def _():
-            direct_recv(slot + 2).wait_recv()
-            forward(slot + 2).start()
-            prepare(slot + 2, saug_a, dens_a)
-
-        apply(saug_b, dens_b)
-        return carry
-
-    def direct_recv(slot):
+                kre[i : i + 16, columns] = re.astype(BF16)
+                kim[i : i + 16, columns] = im.astype(BF16)
+        columns = slice(0, blocks * width)
+        held = dens[pl.ds(first, blocks)].reshape(blocks * width, fields2)
+        acc[at, 0:fields2] += jnp.dot(kre[:, columns], held, preferred_element_type=F32)
+        acc[at, fields2:] += jnp.dot(kim[:, columns], held, preferred_element_type=F32)
+
+    def arrived(slot):
         return pltpu.make_async_remote_copy(
             src_ref=gather.at[0],
             dst_ref=gather.at[slot],
             send_sem=send_sem.at[slot],
             recv_sem=recv_sem.at[slot],
-            device_id=(flip(me, 1), sme),
+            device_id=(flip(me, 2), sme),
             device_id_type=MESH,
         )
 
-    lax.fori_loop(0, n_tgt // 2, pair, 0)
+    prepare(0, 0)
+    hand_on(0)
+    for m in range(3):
+        apply(0, 1, m)
+    arrived(2).wait_recv()
+    prepare(2, 2)
+    hand_on(2)
+
+    def step(q, carry):
+        arrived(2 * q + 2).wait_recv()
+        handed(2 * q - 2)
+        prepare(2 * q + 2, 2 * q + 2)
+        for m in range(3):
+            apply(2 * q - 1, 2, m)
+        hand_on(2 * q + 2)
+        return carry
+
+    lax.fori_loop(1, n_tgt // 2 - 1, step, 0)
 
     def share(bits, m):
         return pltpu.make_async_remote_copy(
@@ -343,8 +340,14 @@
             device_id_type=MESH,
         )
 
+    handed(n_tgt - 4)
     for m in range(3):
-        part[m * tile : (m + 1) * tile, :] = acc[m * tile : (m + 1) * tile, :].astype(BF16)
+        at = slice(m * tile, (m + 1) * tile)
+        apply(n_tgt - 3, 2, m)
+        if m == 0:
+            handed(n_tgt - 2)
+        apply(n_tgt - 1, 1, m)
+        part[at, :] = (acc[at, 0:fields2] + turned(acc[at, fields2:])).astype(BF16)
         for bits in range(1, n_src):
             share(bits, m).start()
 
@@ -356,11 +359,11 @@
         terms += [peers[bits, at, :].astype(F32) for bits in range(1, n_src)]
         while len(terms) > 1:
             terms = [terms[k] + terms[k + 1] for k in range(0, len(terms), 2)]
-        acc[at, :] = terms[0] * scale
-
-    pot[HALO : HALO + rows, :] = acc[0:rows, :] * bw[:, 8:9]
-    pot[HALO + rows : HALO + rows + 8, :] = acc[rows : rows + 8, :] * hw[0:8, 3:4]
-    pot[0:HALO, :] = acc[rows + 8 : rows + 16, :] * hw[8:16, 3:4]
+        acc[at, 0:fields2] = terms[0] * scale
+
+    pot[HALO : HALO + rows, :] = acc[0:rows, 0:fields2] * bw[:, 8:9]
+    pot[HALO + rows : HALO + rows + 8, :] = acc[rows : rows + 8, 0:fields2] * hw[0:8, 3:4]
+    pot[0:HALO, :] = acc[rows + 8 : rows + 16, 0:fields2] * hw[8:16, 3:4]
     for start in range(0, rows, 128):
         value = pot[HALO + start : HALO + start + 128, :]
         for d in range(band_ref.shape[0]):
@@ -368,8 +371,11 @@
             value = value + bw[start : start + 128, d : d + 1] * shifted
         out_ref[start : start + 128, :] = value
 
-    for bits in range(1, n_tgt):
-        direct_recv(bits).wait_send()
+    for bits in range(2, n_tgt, 2):
+        direct(bits).wait_send()
+    for slot in range(0, n_tgt, 2):
+        for copy in forward(slot):
+            copy.wait_send()
     for m in range(3):
         for bits in range(1, n_src):
             share(bits, m).wait_send()
@@ -392,25 +398,28 @@
         in_specs=[vmem] * 7 + [smem, smem, vmem, vmem, smem],
         out_specs=vmem,
         scratch_shapes=[
-            pltpu.VMEM((n_tgt, fields2 + 16 * rounds, rounds * ctrl), BF16),
+            pltpu.VMEM((n_tgt, rounds * (ctrl + 16), fields2), BF16),
             pltpu.VMEM((total, 16), BF16),
             pltpu.VMEM((rows, 16), F32),
             pltpu.VMEM((2, 8, 128), F32),
             pltpu.VMEM((2, 8, 128), F32),
             pltpu.VMEM((16, 8), F32),
-            pltpu.VMEM((16, width), BF16),
-            pltpu.VMEM((16, width), BF16),
-            pltpu.VMEM((fields2, 2 * width), BF16),
-            pltpu.VMEM((fields2, 2 * width), BF16),
-            pltpu.VMEM((total // 3, 2 * width), BF16),
-            pltpu.VMEM((total // 3, 2 * width), BF16),
-            pltpu.VMEM((total // 3, 2 * width), BF16),
-            pltpu.VMEM((total, fields2), F32),
+            pltpu.VMEM((n_tgt, 16, width), BF16),
+            pltpu.VMEM((n_tgt, width, fields2), BF16),
+            pltpu.VMEM((total // 3, 2 * width), BF16),
+            pltpu.VMEM((total // 3, 2 * width), BF16),
+            pltpu.VMEM((total // 3, 2 * width), BF16),
+            pltpu.VMEM((total // 3, 2 * width), BF16),
+            pltpu.VMEM((total // 3, 2 * width), BF16),
+            pltpu.VMEM((total // 3, 2 * width), BF16),
+            pltpu.VMEM((total, 2 * fields2), F32),
             pltpu.VMEM((total, fields2), BF16),
             pltpu.VMEM((n_src, total, fields2), BF16),
             pltpu.VMEM((total, fields2), F32),
             pltpu.SemaphoreType.DMA((n_tgt,)),
             pltpu.SemaphoreType.DMA((n_tgt,)),
+            pltpu.SemaphoreType.DMA((2, n_tgt // 2)),
+            pltpu.SemaphoreType.DMA((2, n_tgt // 2)),
             pltpu.SemaphoreType.DMA((2,)),
             pltpu.SemaphoreType.DMA((2,)),
             pltpu.SemaphoreType.DMA((n_src, 3)),
@@ -429,7 +438,7 @@
         patch,
         patch_factor,
         ctrl_weight,
-        ctrl_coef,
+        jnp.transpose(ctrl_coef, (0, 2, 1)),
         band,
         offsets,
     )

time: 48.9 us -> 47.6 us (0.973)
  Pallas kernels: 46 us -> 40.9 us
  local copies, waits for them, and re-layouts: 2.38 us -> 6.31 us
    pallas_call x1, Pallas kernels: 46 us -> 40.9 us  [per_device(): pl.pallas_call(functools.partial(body, n_tgt, n_src, scale), out_shape=ja...]
    unnamed x24 -> x23, local copies, waits for them, and re-layouts: 2.38 us -> 6.31 us
where the time goes in v1:
time: 47.6 us; the launch traced here: 47.3 us
  Pallas kernels  40.9 us (86%)
  local copies, waits for them, and re-layouts  6.31 us (13%)
    pallas_call x1, Pallas kernels, per_device(): pl.pallas_call(functools.partial(body, n_tgt, n_src, scale), out_shape=ja...  40.9 us
    unnamed x23, local copies, waits for them, and re-layouts  6.31 us

profile of v1, /device:TPU:0, one launch (start us, length us, event | category | flops | bytes accessed | tf_op | source)
XLA Modules:
  0.0 47.3 jit_solution(4352501098094240147)
XLA Ops:
  0.0 0.0 copy-start.1
  0.0 0.7 %copy.13.src_ref = bf16[4,3,128]{2,1,0:T(4,128)(2,1)S(1)} copy(bf16[4,3,128]{2,0,1:T(4,128)(2,1)} %param.14) | data formatting | bytes 6144 | tf_op args[2]
  0.7 0.0 copy-start.2
  0.7 0.0 copy-start.3
  0.7 0.0 copy-start.9
  0.7 0.7 %copy.14.basis_ref = f32[4,3,128]{2,1,0:T(4,128)S(1)} copy(f32[4,3,128]{2,0,1:T(4,128)} %param.16) | data formatting | bytes 12288 | tf_op args[4]
  1.4 0.0 copy-done.1
  1.4 0.0 copy-done.2
  1.5 0.0 copy-done.3
  1.5 0.0 copy-done.9
  1.5 0.0 copy-start
  1.5 0.7 %copy-done = bf16[4,128,32]{1,2,0:T(8,128)(2,1)S(1)} copy-done((bf16[4,128,32]{1,2,0:T(8,128)(2,1)S(1)}, bf16[4,128,32]{1,2,0:T(8,128)(2,1)}, u32[]{:S(2)}) %copy-start) | copy-done | bytes 32792
  2.2 0.0 copy-start.4
  2.2 0.7 %copy-done.4 = f32[512]{0:T(512)S(1)} copy-done((f32[512]{0:T(512)S(1)}, f32[512]{0:T(512)}, u32[]{:S(2)}) %copy-start.4) | copy-done | bytes 2072
  2.9 0.0 copy-start.5
  2.9 0.7 %copy-done.5 = f32[4,128]{1,0:T(4,128)S(1)} copy-done((f32[4,128]{1,0:T(4,128)S(1)}, f32[4,128]{1,0:T(4,128)}, u32[]{:S(2)}) %copy-start.5) | copy-done | bytes 2072
  3.6 0.0 copy-start.6
  3.6 0.7 %copy-done.6 = s32[4,128]{1,0:T(4,128)S(1)} copy-done((s32[4,128]{1,0:T(4,128)S(1)}, s32[4,128]{1,0:T(4,128)}, u32[]{:S(2)}) %copy-start.6) | copy-done | bytes 2072
  4.3 0.0 copy-start.7
  4.3 0.7 %copy-done.7 = s32[4,128]{1,0:T(4,128)S(1)} copy-done((s32[4,128]{1,0:T(4,128)S(1)}, s32[4,128]{1,0:T(4,128)}, u32[]{:S(2)}) %copy-start.7) | copy-done | bytes 2072
  5.0 0.0 copy-start.8
  5.0 0.7 %copy-done.8 = f32[4,32]{1,0:T(4,128)S(1)} copy-done((f32[4,32]{1,0:T(4,128)S(1)}, f32[4,32]{1,0:T(4,128)}, u32[]{:S(2)}) %copy-start.8) | copy-done | bytes 536
  5.6 40.9 %shard_map.118 = f32[512,128]{1,0:T(8,128)S(1)} custom-call(bf16[3,512]{1,0:T(4,128)(2,1)S(1)} %copy-done.2, f32[1,512]{1,0:T(1,128)S(1)} %bitcast.3, bf16[4,3,128]{2,1,0:T(4,128)(2,1)S(1)} %copy.13.src_ref, f32[4,128]{1,0:T(4,128)S(1)} %copy-done.5, f32[4,3,128]{2,1,0:T(4,128)S(1)} %copy.14.basis_ref, s32[4,128]{1,0:T(4,128)S(1)} %copy-done.6, ...), custom_call_target="tpu_custom_call" | custom-call | tf_op jit(solution)/shard_map/pallas_call | solution.py:395
  46.6 0.7 %copy.16 = f32[512,128]{1,0:T(8,128)} copy(f32[512,128]{1,0:T(8,128)S(1)} %shard_map.118) | data formatting | bytes 524288
Async XLA Ops:
  0.0 1.4 %copy-start.1 = (f32[8,512]{1,0:T(8,128)S(1)}, f32[8,512]{1,0:T(8,128)}, u32[]{:S(2)}) copy-start(f32[8,512]{1,0:T(8,128)} %band_ref.1) | copy-start | bytes 49156
  0.7 0.7 %copy-start.2 = (bf16[3,512]{1,0:T(4,128)(2,1)S(1)}, bf16[3,512]{1,0:T(4,128)(2,1)}, u32[]{:S(2)}) copy-start(bf16[3,512]{1,0:T(4,128)(2,1)} %tgt_ref.1) | copy-start | bytes 9220
  0.7 0.7 %copy-start.3 = (f32[4,2,4]{2,1,0:T(2,128)S(1)}, f32[4,2,4]{2,1,0:T(2,128)}, u32[]{:S(2)}) copy-start(f32[4,2,4]{2,1,0:T(2,128)} %pf_ref.1) | copy-start | bytes 388
  0.7 0.8 %copy-start.9 = (s32[8]{0:T(128)S(1)}, s32[8]{0:T(128)}, u32[]{:S(2)}) copy-start(s32[8]{0:T(128)} %off_ref.1) | copy-start | bytes 100
  1.5 0.8 %copy-start = (bf16[4,128,32]{1,2,0:T(8,128)(2,1)S(1)}, bf16[4,128,32]{1,2,0:T(8,128)(2,1)}, u32[]{:S(2)}) copy-start(bf16[4,128,32]{1,2,0:T(8,128)(2,1)} %param.21) | copy-start | bytes 98308
  2.2 0.7 %copy-start.4 = (f32[512]{0:T(512)S(1)}, f32[512]{0:T(512)}, u32[]{:S(2)}) copy-start(f32[512]{0:T(512)} %param.13) | copy-start | bytes 6148
  2.9 0.7 %copy-start.5 = (f32[4,128]{1,0:T(4,128)S(1)}, f32[4,128]{1,0:T(4,128)}, u32[]{:S(2)}) copy-start(f32[4,128]{1,0:T(4,128)} %sw_ref.1) | copy-start | bytes 6148
  3.6 0.7 %copy-start.6 = (s32[4,128]{1,0:T(4,128)S(1)}, s32[4,128]{1,0:T(4,128)}, u32[]{:S(2)}) copy-start(s32[4,128]{1,0:T(4,128)} %span_ref.1) | copy-start | bytes 6148
  4.3 0.7 %copy-start.7 = (s32[4,128]{1,0:T(4,128)S(1)}, s32[4,128]{1,0:T(4,128)}, u32[]{:S(2)}) copy-start(s32[4,128]{1,0:T(4,128)} %patch_ref.1) | copy-start | bytes 6148
  5.0 0.7 %copy-start.8 = (f32[4,32]{1,0:T(4,128)S(1)}, f32[4,32]{1,0:T(4,128)}, u32[]{:S(2)}) copy-start(f32[4,32]{1,0:T(4,128)} %cw_ref.1) | copy-start | bytes 1540
